TPU v7x, 32 devices: a whole 2x2x4 slice. The times are simulated.
32 devices in a mesh: mem: 4 (over z), lon: 8 (over y, x, core).
Axes of the slice: x: 2, y: 2, z: 4, core: 2. Of those that a mesh axis runs over, the one named last changes fastest.
Arguments:
- fields: bfloat16 [20, 64, 64, 128], P('mem', None, 'lon'), may hold values from -8 to 8
- w_query: bfloat16 [24, 576], replicated, may hold values from -1 to 1
- w_key: bfloat16 [24, 576], replicated, may hold values from -1 to 1
- w_value: bfloat16 [24, 576], replicated, may hold values from -0.25 to 0.25
- w_out: bfloat16 [64, 216], replicated, may hold values from -1.25 to 1.25
Outputs:
- updated: bfloat16 [20, 64, 64, 128], P('mem', None, 'lon')
All inputs are finite; a program needn't handle non-finite values.
Results may differ from a plain program's by a relative error of at most 0.008.
Values may be sent and summed in bfloat16 or wider, within the bound.
A program may use at most 64 MiB of HBM per device.

v0:
```python
import functools
import math

import jax
import jax.numpy as jnp
from jax import lax
from jax.experimental import pallas as pl
from jax.experimental.pallas import tpu as pltpu
from jax.sharding import PartitionSpec as P

MESH = pl.DeviceIdType.MESH
F32 = jnp.float32
BF16 = jnp.bfloat16


def with_halo(block, sides, width):
    for axis, dim in sides:
        count = lax.axis_size(axis)
        forward = [(i, i + 1) for i in range(count - 1)]
        forward.append((count - 1, 0))
        backward = [(target, source) for source, target in forward]
        low = lax.ppermute(
            lax.slice_in_dim(block, block.shape[dim] - width, None, axis=dim), axis, forward
        )
        high = lax.ppermute(lax.slice_in_dim(block, 0, width, axis=dim), axis, backward)
        block = jnp.concatenate([low, block, high], axis=dim)
    return block


def tap_stack(extended):
    span_lon = extended.shape[2] - 2
    latitudes = extended.shape[3]
    padded = jnp.pad(extended, ((0, 0), (0, 0), (0, 0), (1, 1)))
    return jnp.concatenate(
        [
            padded[:, :, lon_step : lon_step + span_lon, lat_step : lat_step + latitudes]
            for lon_step in range(3)
            for lat_step in range(3)
        ],
        axis=1,
    )


def plain_shards(fields, w_query, w_key, w_value, w_out):
    members = fields.shape[0]
    longitudes = fields.shape[2]
    latitudes = fields.shape[3]
    inner_width = w_query.shape[0]
    extended = with_halo(fields, (("lon", 2),), 1)
    w_inner = jnp.concatenate([w_query, w_key, w_value], axis=0)
    projected = jnp.einsum(
        "oc,mcwh->mowh", w_inner, tap_stack(extended), preferred_element_type=jnp.float32
    ).astype(jnp.bfloat16)
    queries = projected[:, :inner_width]
    keys_local = projected[:, inner_width : 2 * inner_width]
    values = projected[:, 2 * inner_width :]
    query_blocks, key_blocks = (
        lax.all_to_all(queries, "mem", split_axis=3, concat_axis=0, tiled=True),
        lax.all_to_all(keys_local, "mem", split_axis=3, concat_axis=0, tiled=True),
    )
    total_members = query_blocks.shape[0]
    partial_value = jnp.dot(
        query_blocks.reshape(total_members, -1),
        key_blocks.reshape(total_members, -1).T,
        preferred_element_type=jnp.float32,
    )
    score_scale = 1.0 / math.sqrt(inner_width * latitudes * longitudes * lax.axis_size("lon"))
    first_row = lax.axis_index("mem") * members
    gram_sums = lax.psum(partial_value, ("mem", "lon"))
    weights_all = jax.nn.softmax(gram_sums * score_scale, axis=1).astype(jnp.bfloat16)
    weights_own = lax.dynamic_slice_in_dim(weights_all, first_row, members, 0)
    mixed_values = jnp.einsum(
        "mn,ncwh->mcwh",
        weights_own,
        lax.all_gather(values, "mem", axis=0, tiled=True),
        preferred_element_type=jnp.float32,
    ).astype(jnp.bfloat16)
    mixed_ext = with_halo(mixed_values, (("lon", 2),), 1)
    branch = jnp.einsum(
        "oc,mcwh->mowh", w_out, tap_stack(mixed_ext), preferred_element_type=jnp.float32
    )
    return (fields.astype(jnp.float32) + branch).astype(jnp.bfloat16)


def lat_taps(block, lat):
    width = block.shape[1]
    lane = lax.broadcasted_iota(jnp.int32, block.shape, 1) & (lat - 1)
    low = jnp.where(lane == 0, 0.0, pltpu.roll(block, 1, 1))
    high = jnp.where(lane == lat - 1, 0.0, pltpu.roll(block, width - 1, 1))
    return jnp.concatenate([low, block, high], axis=0).astype(BF16)


def shifted_sum(taps_out, rows, lat):
    zero = jnp.zeros((rows, lat), F32)
    return (
        taps_out[rows : 2 * rows]
        + jnp.concatenate([zero, taps_out[:rows, :-lat]], axis=1)
        + jnp.concatenate([taps_out[2 * rows :, lat:], zero], axis=1)
    )


def layer_kernel(
    dims, f_ref, wq_ref, wk_ref, wv_ref, w_out_ref, out_ref,
    wi_ref, wo_ref, y_ref, halo, v_raw, qk_edge, qk_out, qk_all, v_all, g_out, g_mem, g_lon, edge_out, edge_in,
    halo_s, halo_r, qk_s, qk_r, v_s, v_r, gm_s, gm_r, gl_s, gl_r, edge_s, edge_r,
):
    mems, lons, members, ch, cq, cols, lat, score_scale = dims
    wide = cols * lat
    piece = wide // mems
    total = mems * members
    steps = cols // 2
    inner = 3 * cq
    z = lax.axis_index("mem")
    s = lax.axis_index("lon")
    right = lax.rem(s + 1, lons)
    left = lax.rem(s + lons - 1, lons)

    def mem_peer(d):
        return lax.rem(z + d, mems)

    def lon_peer(d):
        return lax.rem(s + d, lons)

    by_distance = [
        sorted([p for p in range(mems) if p != home], key=lambda p, home=home: (-abs(p - home), p))
        for home in range(mems)
    ]

    def far_peer(k):
        peer = by_distance[0][k]
        for home in range(1, mems):
            peer = jnp.where(z == home, by_distance[home][k], peer)
        return peer

    barrier = pltpu.get_barrier_semaphore()
    for d in range(1, mems):
        pl.semaphore_signal(barrier, inc=1, device_id={"mem": mem_peer(d)}, device_id_type=MESH)
    for d in range(1, lons):
        pl.semaphore_signal(barrier, inc=1, device_id={"lon": lon_peer(d)}, device_id_type=MESH)
    w_inner = jnp.concatenate([ref[...].astype(F32) for ref in (wq_ref, wk_ref, wv_ref)], axis=0)
    w_outer = w_out_ref[...].astype(F32)
    wi_ref[...] = jnp.concatenate([w_inner[:, a * 3 * ch : (a + 1) * 3 * ch] for a in range(3)], axis=0).astype(BF16)
    wo_ref[...] = jnp.concatenate([w_outer[:, a * 3 * cq : (a + 1) * 3 * cq] for a in range(3)], axis=0).astype(BF16)
    pl.semaphore_wait(barrier, mems + lons - 2)

    def remote(src, dst, send, recv, device):
        return pltpu.make_async_remote_copy(
            src_ref=src, dst_ref=dst, send_sem=send, recv_sem=recv, device_id=device, device_id_type=MESH
        )

    halo_copies = [
        remote(f_ref.at[:, :, pl.ds(wide - lat, lat)], halo.at[0], halo_s.at[0], halo_r.at[0], {"lon": right}),
        remote(f_ref.at[:, :, pl.ds(0, lat)], halo.at[1], halo_s.at[1], halo_r.at[1], {"lon": left}),
    ]
    for copy in halo_copies:
        copy.start()

    qk_copies = [remote(qk_out.at[p], qk_all.at[z], qk_s.at[p], qk_r.at[z], {"mem": p}) for p in range(mems)]
    for m in range(members):
        taps = lat_taps(f_ref[m].astype(F32), lat)
        projected = shifted_sum(jnp.dot(wi_ref[...], taps, preferred_element_type=F32), inner, lat)
        queries_keys = projected[: 2 * cq]
        v_raw[m] = projected[2 * cq :]
        qk_edge[0, m] = queries_keys[:, :lat]
        qk_edge[1, m] = queries_keys[:, wide - lat :]
        for p in range(mems):
            qk_out[p, m] = queries_keys[:, p * piece : (p + 1) * piece].astype(BF16)
        for p in range(1, mems - 1):
            @pl.when(z != p)
            def _(p=p, m=m):
                remote(qk_out.at[p, m], qk_all.at[z, m], qk_s.at[p], qk_r.at[z], {"mem": p}).start()
    for copy in halo_copies:
        copy.wait_recv()
    beside = []
    for side, rows in ((0, slice(0, inner)), (1, slice(2 * inner, 3 * inner))):
        columns = jnp.concatenate([halo[side, m] for m in range(members)], axis=1).astype(F32)
        beside.append(jnp.dot(wi_ref[rows], lat_taps(columns, lat), preferred_element_type=F32))
    for m in range(members):
        lanes = slice(m * lat, (m + 1) * lat)
        qk_out[0, m, :, :lat] = (qk_edge[0, m] + beside[0][: 2 * cq, lanes]).astype(BF16)
        qk_out[mems - 1, m, :, piece - lat :] = (qk_edge[1, m] + beside[1][: 2 * cq, lanes]).astype(BF16)
    for p in (0, mems - 1):
        @pl.when(z != p)
        def _(p=p):
            qk_copies[p].start()
    for m in range(members):
        lanes = slice(m * lat, (m + 1) * lat)
        for t in range(steps):
            upper = v_raw[m, :, t * lat : (t + 1) * lat]
            lower = v_raw[m, :, (steps + t) * lat : (steps + t + 1) * lat]
            if t == 0:
                upper = upper + beside[0][2 * cq :, lanes]
            if t == steps - 1:
                lower = lower + beside[1][2 * cq :, lanes]
            v_all[t, z, m] = jnp.concatenate([upper, lower], axis=0).astype(BF16)
    order = [0, steps - 1] + list(range(1, steps - 1))
    v_copies = {}
    for t in order:
        for k in range(mems - 1):
            v_copies[t, k] = remote(
                v_all.at[t, z], v_all.at[t, z], v_s.at[t, k], v_r.at[t, z], {"mem": far_peer(k)}
            )
    for k in range(mems - 1):
        peer = far_peer(k)
        remote(qk_out.at[peer], qk_all.at[z], qk_s.at[peer], qk_r.at[z], {"mem": peer}).wait_send()
        v_copies[order[0], k].start()

    qk_all[z] = qk_out[z]
    column = lax.broadcasted_iota(jnp.int32, (cq, total * cq), 1).astype(F32)
    row = lax.broadcasted_iota(jnp.int32, (cq, total * cq), 0).astype(F32)
    same = jnp.where(column - cq * jnp.floor((column + 0.5) / cq) == row, 1.0, 0.0)
    spread = lax.broadcasted_iota(jnp.int32, (total * cq, 128), 0) - cq * lax.broadcasted_iota(
        jnp.int32, (total * cq, 128), 1
    )
    groups = jnp.where((spread >= 0) & (spread < cq), 1.0, 0.0)
    for d in range(1, mems):
        source = mem_peer(d)
        remote(qk_out.at[source], qk_all.at[source], qk_s.at[source], qk_r.at[source], {"mem": source}).wait_recv()
    both = qk_all[...].astype(F32).reshape(total, 2 * cq, piece)
    queries = both[:, :cq].reshape(total * cq, piece).astype(BF16)
    keys = both[:, cq:].reshape(total * cq, piece).astype(BF16)
    products = lax.dot_general(queries, keys, (((1,), (1,)), ((), ())), preferred_element_type=F32)
    by_member = jnp.sum(products.reshape(total, cq, total * cq) * same[None], axis=1)
    gram = jnp.dot(by_member, groups, precision=lax.Precision.HIGHEST, preferred_element_type=F32)
    filler = jnp.zeros((8 - members, 128), F32)
    for p in range(mems):
        g_out[p] = jnp.concatenate([gram[p * members : (p + 1) * members], filler], axis=0)
    gm_copies = [
        remote(g_out.at[mem_peer(d)], g_mem.at[z], gm_s.at[d - 1], gm_r.at[d - 1], {"mem": mem_peer(d)})
        for d in range(1, mems)
    ]
    for copy in gm_copies:
        copy.start()
    for t in order[1:]:
        for k in range(mems - 1):
            v_copies[t, k].start()
    g_mem[z] = g_out[z]
    for copy in gm_copies:
        copy.wait_recv()
    g_lon[s] = jnp.sum(g_mem[...], axis=0)
    gl_copies = [
        remote(g_lon.at[s], g_lon.at[s], gl_s.at[d - 1], gl_r.at[d - 1], {"lon": lon_peer(d)})
        for d in range(1, lons)
    ]
    for copy in gl_copies:
        copy.start()
    for copy in gl_copies:
        copy.wait_recv()
    lane = lax.broadcasted_iota(jnp.int32, (8, 128), 1)
    scores = jnp.where(lane < total, jnp.sum(g_lon[...], axis=0) * score_scale, -jnp.inf)
    powers = jnp.exp(scores - jnp.max(scores, axis=1, keepdims=True))
    weights = (powers / jnp.sum(powers, axis=1, keepdims=True)).astype(BF16).astype(F32)

    edge_copies = [
        remote(edge_out.at[0], edge_in.at[0], edge_s.at[0], edge_r.at[0], {"lon": right}),
        remote(edge_out.at[1], edge_in.at[1], edge_s.at[1], edge_r.at[1], {"lon": left}),
    ]
    edge_pad = jnp.zeros((edge_out.shape[2] - cq, lat), F32)
    for t in order:
        for d in range(1, mems):
            source = mem_peer(d)
            remote(v_all.at[t, source], v_all.at[t, source], v_s.at[t, 0], v_r.at[t, source], {"mem": source}).wait_recv()
        sums = [None] * members
        for n in range(total):
            block = v_all[t, n // members, n % members].astype(F32)
            for m in range(members):
                term = weights[m : m + 1, n : n + 1] * block
                sums[m] = term if n == 0 else sums[m] + term
        rounded = [sums[m].astype(BF16).astype(F32) for m in range(members)]
        if t == 0:
            for m in range(members):
                edge_out[1, m] = jnp.concatenate([rounded[m][:cq], edge_pad], axis=0).astype(BF16)
            edge_copies[1].start()
        if t == steps - 1:
            for m in range(members):
                edge_out[0, m] = jnp.concatenate([rounded[m][cq:], edge_pad], axis=0).astype(BF16)
            edge_copies[0].start()
        columns = jnp.concatenate([r[:cq] for r in rounded] + [r[cq:] for r in rounded], axis=1)
        y_ref[t] = jnp.dot(wo_ref[...], lat_taps(columns, lat), preferred_element_type=F32)
    for copy in edge_copies:
        copy.wait_recv()
    beside = []
    for side, rows in ((0, slice(0, ch)), (1, slice(2 * ch, 3 * ch))):
        columns = jnp.concatenate([edge_in[side, m].astype(F32)[:cq] for m in range(members)], axis=1)
        beside.append(jnp.dot(wo_ref[rows], lat_taps(columns, lat), preferred_element_type=F32))
    for m in range(members):
        def column_taps(tap, i):
            if i < 0 or i >= cols:
                return beside[0 if i < 0 else 1][:, m * lat : (m + 1) * lat]
            first = ((i // steps) * members + m) * lat
            return y_ref[i % steps, tap * ch : (tap + 1) * ch, first : first + lat]

        for i in range(cols):
            lanes = slice(i * lat, (i + 1) * lat)
            branch = column_taps(1, i) + column_taps(0, i - 1) + column_taps(2, i + 1)
            out_ref[m, :, lanes] = (f_ref[m, :, lanes].astype(F32) + branch).astype(BF16)
    for copy in halo_copies + list(v_copies.values()) + gm_copies + gl_copies + edge_copies:
        copy.wait_send()


def shards(mems, lons, fields, w_query, w_key, w_value, w_out):
    members, ch, cols, lat = fields.shape
    cq = w_query.shape[0]
    wide = cols * lat
    if cols % mems or cols % 2 or cols < 4 or mems < 2 or lat != 128 or members > 8 or (2 * cq) % 16 or ch % 16:
        return plain_shards(fields, w_query, w_key, w_value, w_out)
    score_scale = 1.0 / math.sqrt(cq * lat * cols * lons)
    dims = (mems, lons, members, ch, cq, cols, lat, score_scale)
    edge_rows = -(-cq // 16) * 16
    dma = pltpu.SemaphoreType.DMA
    vmem = pl.BlockSpec(memory_space=pltpu.VMEM)
    updated = pl.pallas_call(
        functools.partial(layer_kernel, dims),
        out_shape=jax.ShapeDtypeStruct((members, ch, wide), BF16),
        in_specs=[vmem] * 5,
        out_specs=vmem,
        scratch_shapes=[
            pltpu.VMEM((9 * cq, 3 * ch), BF16),
            pltpu.VMEM((3 * ch, 3 * cq), BF16),
            pltpu.VMEM((cols // 2, 3 * ch, 2 * members * lat), F32),
            pltpu.VMEM((2, members, ch, lat), BF16),
            pltpu.VMEM((members, cq, wide), F32),
            pltpu.VMEM((2, members, 2 * cq, lat), F32),
            pltpu.VMEM((mems, members, 2 * cq, wide // mems), BF16),
            pltpu.VMEM((mems, members, 2 * cq, wide // mems), BF16),
            pltpu.VMEM((cols // 2, mems, members, 2 * cq, lat), BF16),
            pltpu.VMEM((mems, 8, 128), F32),
            pltpu.VMEM((mems, 8, 128), F32),
            pltpu.VMEM((lons, 8, 128), F32),
            pltpu.VMEM((2, members, edge_rows, lat), BF16),
            pltpu.VMEM((2, members, edge_rows, lat), BF16),
            dma((2,)), dma((2,)),
            dma((mems,)), dma((mems,)),
            dma((cols // 2, mems - 1)), dma((cols // 2, mems)),
            dma((mems - 1,)), dma((mems - 1,)),
            dma((lons - 1,)), dma((lons - 1,)),
            dma((2,)), dma((2,)),
        ],
        compiler_params=pltpu.CompilerParams(
            collective_id=0, has_side_effects=True, vmem_limit_bytes=40 * 1024 * 1024
        ),
    )(fields.reshape(members, ch, wide), w_query, w_key, w_value, w_out)
    return updated.reshape(members, ch, cols, lat)


def solution(mesh):
    return jax.shard_map(
        functools.partial(shards, mesh.shape["mem"], mesh.shape["lon"]),
        mesh=mesh,
        in_specs=(P("mem", None, "lon", None), P(), P(), P(), P()),
        out_specs=P("mem", None, "lon", None),
        check_vma=False,
    )
```

profile of v0, /device:TPU:0, one launch (start us, length us, event | category | flops | bytes accessed | tf_op | source)
XLA Modules:
  0.0 43.3 jit_solution(6476922377480426266)
XLA Ops:
  0.0 0.0 copy-start
  0.0 0.0 copy-start.3
  0.0 0.0 copy-start.2
  0.0 0.0 copy-start.1
  0.0 1.4 %reshape.6.f_ref = bf16[5,64,1024]{2,1,0:T(8,128)(2,1)S(1)} reshape(bf16[5,64,8,128]{3,2,1,0:T(8,128)(2,1)} %param.5) | data formatting | bytes 1310720 | tf_op jit(solution)/shard_map/reshape | solution.py:342
  1.4 0.0 copy-done
  1.4 0.0 copy-done.3
  1.4 0.0 copy-done.2
  1.4 0.0 copy-done.1
  1.4 40.8 %shard_map.55 = bf16[5,64,1024]{2,1,0:T(8,128)(2,1)S(1)} custom-call(bf16[5,64,1024]{2,1,0:T(8,128)(2,1)S(1)} %reshape.6.f_ref, bf16[24,576]{1,0:T(8,128)(2,1)S(1)} %copy-done.1, bf16[24,576]{1,0:T(8,128)(2,1)S(1)} %copy-done.2, bf16[24,576]{1,0:T(8,128)(2,1)S(1)} %copy-done.3, bf16[64,216]{1,0:T(8,128)(2,1)S(1)} %copy-done), custom_call_target="tpu_custom_call" | custom-call | tf_op jit(solution)/shard_map/pallas_call | solution.py:312
  42.3 1.0 %copy.6 = bf16[40,8,8,128]{3,2,1,0:T(8,128)(2,1)} copy(bf16[40,8,8,128]{3,1,2,0:T(8,128)(2,1)S(1)} %bitcast.6) | data formatting | bytes 1310720
Async XLA Ops:
  0.0 1.4 %copy-start = (bf16[64,216]{1,0:T(8,128)(2,1)S(1)}, bf16[64,216]{1,0:T(8,128)(2,1)}, u32[]{:S(2)}) copy-start(bf16[64,216]{1,0:T(8,128)(2,1)} %w_out_ref.1) | copy-start | bytes 82948
  0.0 1.4 %copy-start.3 = (bf16[24,576]{1,0:T(8,128)(2,1)S(1)}, bf16[24,576]{1,0:T(8,128)(2,1)}, u32[]{:S(2)}) copy-start(bf16[24,576]{1,0:T(8,128)(2,1)} %wv_ref.1) | copy-start | bytes 82948
  0.0 1.4 %copy-start.2 = (bf16[24,576]{1,0:T(8,128)(2,1)S(1)}, bf16[24,576]{1,0:T(8,128)(2,1)}, u32[]{:S(2)}) copy-start(bf16[24,576]{1,0:T(8,128)(2,1)} %wk_ref.1) | copy-start | bytes 82948
  0.0 1.4 %copy-start.1 = (bf16[24,576]{1,0:T(8,128)(2,1)S(1)}, bf16[24,576]{1,0:T(8,128)(2,1)}, u32[]{:S(2)}) copy-start(bf16[24,576]{1,0:T(8,128)(2,1)} %wq_ref.1) | copy-start | bytes 82948
where the time goes:
time: 43.4 us; the launch traced here: 43.3 us
  Pallas kernels  40.8 us (94%)
  local copies, waits for them, and re-layouts  2.36 us (5%)
    pallas_call x1, Pallas kernels, shards(): pl.pallas_call(functools.partial(layer_kernel, dims), out_shape=jax.Shape...  40.8 us
    reshape x1, local copies, waits for them, and re-layouts, shards(): fields.reshape(members, ch, wide)  1.39 us
    unnamed x9, local copies, waits for them, and re-layouts  0.98 us

commit v1 on v0

--- a/solution.py
+++ b/solution.py
@@ -101,12 +101,13 @@
 
 def layer_kernel(
     dims, f_ref, wq_ref, wk_ref, wv_ref, w_out_ref, out_ref,
-    wi_ref, wo_ref, y_ref, halo, v_raw, qk_edge, qk_out, qk_all, v_all, g_out, g_mem, g_lon, edge_out, edge_in,
+    wi_ref, wo_ref, y_ref, halo, v_raw, qk_edge, by_member, qk_out, qk_all, v_all, g_out, g_mem, g_lon, edge_out, edge_in,
     halo_s, halo_r, qk_s, qk_r, v_s, v_r, gm_s, gm_r, gl_s, gl_r, edge_s, edge_r,
 ):
     mems, lons, members, ch, cq, cols, lat, score_scale = dims
     wide = cols * lat
-    piece = wide // mems
+    slots = cols // 2 - 1
+    is_inner = (lax.axis_index("mem") > 0) & (lax.axis_index("mem") < mems - 1)
     total = mems * members
     steps = cols // 2
     inner = 3 * cq
@@ -155,7 +156,11 @@
     for copy in halo_copies:
         copy.start()
 
-    qk_copies = [remote(qk_out.at[p], qk_all.at[z], qk_s.at[p], qk_r.at[z], {"mem": p}) for p in range(mems)]
+    def qk_copy(p):
+        if 0 < p < mems - 1:
+            return remote(qk_out.at[p], qk_all.at[z], qk_s.at[p], qk_r.at[z], {"mem": p})
+        return remote(qk_out.at[p, 0], qk_all.at[z, 0], qk_s.at[p], qk_r.at[z], {"mem": p})
+
     for m in range(members):
         taps = lat_taps(f_ref[m].astype(F32), lat)
         projected = shifted_sum(jnp.dot(wi_ref[...], taps, preferred_element_type=F32), inner, lat)
@@ -163,12 +168,12 @@
         v_raw[m] = projected[2 * cq :]
         qk_edge[0, m] = queries_keys[:, :lat]
         qk_edge[1, m] = queries_keys[:, wide - lat :]
-        for p in range(mems):
-            qk_out[p, m] = queries_keys[:, p * piece : (p + 1) * piece].astype(BF16)
+        for i in range(1, cols - 1):
+            qk_out[1 + (i - 1) // slots, (i - 1) % slots, m] = queries_keys[:, i * lat : (i + 1) * lat].astype(BF16)
         for p in range(1, mems - 1):
             @pl.when(z != p)
             def _(p=p, m=m):
-                remote(qk_out.at[p, m], qk_all.at[z, m], qk_s.at[p], qk_r.at[z], {"mem": p}).start()
+                remote(qk_out.at[p, :, m], qk_all.at[z, :, m], qk_s.at[p], qk_r.at[z], {"mem": p}).start()
     for copy in halo_copies:
         copy.wait_recv()
     beside = []
@@ -177,12 +182,12 @@
         beside.append(jnp.dot(wi_ref[rows], lat_taps(columns, lat), preferred_element_type=F32))
     for m in range(members):
         lanes = slice(m * lat, (m + 1) * lat)
-        qk_out[0, m, :, :lat] = (qk_edge[0, m] + beside[0][: 2 * cq, lanes]).astype(BF16)
-        qk_out[mems - 1, m, :, piece - lat :] = (qk_edge[1, m] + beside[1][: 2 * cq, lanes]).astype(BF16)
+        qk_out[0, 0, m] = (qk_edge[0, m] + beside[0][: 2 * cq, lanes]).astype(BF16)
+        qk_out[mems - 1, 0, m] = (qk_edge[1, m] + beside[1][: 2 * cq, lanes]).astype(BF16)
     for p in (0, mems - 1):
         @pl.when(z != p)
         def _(p=p):
-            qk_copies[p].start()
+            qk_copy(p).start()
     for m in range(members):
         lanes = slice(m * lat, (m + 1) * lat)
         for t in range(steps):
@@ -201,11 +206,8 @@
                 v_all.at[t, z], v_all.at[t, z], v_s.at[t, k], v_r.at[t, z], {"mem": far_peer(k)}
             )
     for k in range(mems - 1):
-        peer = far_peer(k)
-        remote(qk_out.at[peer], qk_all.at[z], qk_s.at[peer], qk_r.at[z], {"mem": peer}).wait_send()
         v_copies[order[0], k].start()
 
-    qk_all[z] = qk_out[z]
     column = lax.broadcasted_iota(jnp.int32, (cq, total * cq), 1).astype(F32)
     row = lax.broadcasted_iota(jnp.int32, (cq, total * cq), 0).astype(F32)
     same = jnp.where(column - cq * jnp.floor((column + 0.5) / cq) == row, 1.0, 0.0)
@@ -213,15 +215,33 @@
         jnp.int32, (total * cq, 128), 1
     )
     groups = jnp.where((spread >= 0) & (spread < cq), 1.0, 0.0)
-    for d in range(1, mems):
-        source = mem_peer(d)
-        remote(qk_out.at[source], qk_all.at[source], qk_s.at[source], qk_r.at[source], {"mem": source}).wait_recv()
-    both = qk_all[...].astype(F32).reshape(total, 2 * cq, piece)
-    queries = both[:, :cq].reshape(total * cq, piece).astype(BF16)
-    keys = both[:, cq:].reshape(total * cq, piece).astype(BF16)
-    products = lax.dot_general(queries, keys, (((1,), (1,)), ((), ())), preferred_element_type=F32)
-    by_member = jnp.sum(products.reshape(total, cq, total * cq) * same[None], axis=1)
-    gram = jnp.dot(by_member, groups, precision=lax.Precision.HIGHEST, preferred_element_type=F32)
+    def add_columns(first, count):
+        parts = [qk_all[:, first + j].astype(F32).reshape(total, 2 * cq, lat) for j in range(count)]
+        both = jnp.concatenate(parts, axis=2)
+        queries = both[:, :cq].reshape(total * cq, count * lat).astype(BF16)
+        keys = both[:, cq:].reshape(total * cq, count * lat).astype(BF16)
+        products = lax.dot_general(queries, keys, (((1,), (1,)), ((), ())), preferred_element_type=F32)
+        return jnp.sum(products.reshape(total, cq, total * cq) * same[None], axis=1)
+
+    @pl.when(is_inner)
+    def _():
+        qk_all[z] = qk_out[z]
+        for d in range(1, mems):
+            source = mem_peer(d)
+            remote(qk_out.at[source], qk_all.at[source], qk_s.at[0], qk_r.at[source], {"mem": source}).wait_recv()
+        by_member[...] = add_columns(0, slots)
+
+    @pl.when(jnp.logical_not(is_inner))
+    def _():
+        qk_all[z, 0] = qk_out[z, 0]
+        for d in range(1, mems):
+            source = mem_peer(d)
+            remote(
+                qk_out.at[source, 0], qk_all.at[source, 0], qk_s.at[0], qk_r.at[source], {"mem": source}
+            ).wait_recv()
+        by_member[...] = add_columns(0, 1)
+
+    gram = jnp.dot(by_member[...], groups, precision=lax.Precision.HIGHEST, preferred_element_type=F32)
     filler = jnp.zeros((8 - members, 128), F32)
     for p in range(mems):
         g_out[p] = jnp.concatenate([gram[p * members : (p + 1) * members], filler], axis=0)
@@ -294,6 +314,10 @@
             lanes = slice(i * lat, (i + 1) * lat)
             branch = column_taps(1, i) + column_taps(0, i - 1) + column_taps(2, i + 1)
             out_ref[m, :, lanes] = (f_ref[m, :, lanes].astype(F32) + branch).astype(BF16)
+    for p in range(mems):
+        @pl.when(z != p)
+        def _(p=p):
+            qk_copy(p).wait_send()
     for copy in halo_copies + list(v_copies.values()) + gm_copies + gl_copies + edge_copies:
         copy.wait_send()
 
@@ -302,7 +326,7 @@
     members, ch, cols, lat = fields.shape
     cq = w_query.shape[0]
     wide = cols * lat
-    if cols % mems or cols % 2 or cols < 4 or mems < 2 or lat != 128 or members > 8 or (2 * cq) % 16 or ch % 16:
+    if mems != 4 or cols % 2 or cols < 4 or lat != 128 or members > 8 or (2 * cq) % 16 or ch % 16:
         return plain_shards(fields, w_query, w_key, w_value, w_out)
     score_scale = 1.0 / math.sqrt(cq * lat * cols * lons)
     dims = (mems, lons, members, ch, cq, cols, lat, score_scale)
@@ -321,8 +345,9 @@
             pltpu.VMEM((2, members, ch, lat), BF16),
             pltpu.VMEM((members, cq, wide), F32),
             pltpu.VMEM((2, members, 2 * cq, lat), F32),
-            pltpu.VMEM((mems, members, 2 * cq, wide // mems), BF16),
-            pltpu.VMEM((mems, members, 2 * cq, wide // mems), BF16),
+            pltpu.VMEM((mems * members, mems * members * cq), F32),
+            pltpu.VMEM((mems, cols // 2 - 1, members, 2 * cq, lat), BF16),
+            pltpu.VMEM((mems, cols // 2 - 1, members, 2 * cq, lat), BF16),
             pltpu.VMEM((cols // 2, mems, members, 2 * cq, lat), BF16),
             pltpu.VMEM((mems, 8, 128), F32),
             pltpu.VMEM((mems, 8, 128), F32),

time: 43.4 us -> 43.1 us (level)
  no operation moved by 1% of the time
where the time goes in v1:
time: 43.1 us; the launch traced here: 43 us
  Pallas kernels  40.6 us (94%)
  local copies, waits for them, and re-layouts  2.36 us (5%)
    pallas_call x1, Pallas kernels, shards(): pl.pallas_call(functools.partial(layer_kernel, dims), out_shape=jax.Shape...  40.6 us
    reshape x1, local copies, waits for them, and re-layouts, shards(): fields.reshape(members, ch, wide)  1.39 us
    unnamed x9, local copies, waits for them, and re-layouts  0.98 us

profile of v1, /device:TPU:0, one launch (start us, length us, event | category | flops | bytes accessed | tf_op | source)
XLA Modules:
  0.0 43.0 jit_solution(16516169717675862323)
XLA Ops:
  0.0 0.0 copy-start
  0.0 0.0 copy-start.3
  0.0 0.0 copy-start.2
  0.0 0.0 copy-start.1
  0.0 1.4 %reshape.6.f_ref = bf16[5,64,1024]{2,1,0:T(8,128)(2,1)S(1)} reshape(bf16[5,64,8,128]{3,2,1,0:T(8,128)(2,1)} %param.5) | data formatting | bytes 1310720 | tf_op jit(solution)/shard_map/reshape | solution.py:367
  1.4 0.0 copy-done
  1.4 0.0 copy-done.3
  1.4 0.0 copy-done.2
  1.4 0.0 copy-done.1
  1.4 40.6 %shard_map.55 = bf16[5,64,1024]{2,1,0:T(8,128)(2,1)S(1)} custom-call(bf16[5,64,1024]{2,1,0:T(8,128)(2,1)S(1)} %reshape.6.f_ref, bf16[24,576]{1,0:T(8,128)(2,1)S(1)} %copy-done.1, bf16[24,576]{1,0:T(8,128)(2,1)S(1)} %copy-done.2, bf16[24,576]{1,0:T(8,128)(2,1)S(1)} %copy-done.3, bf16[64,216]{1,0:T(8,128)(2,1)S(1)} %copy-done), custom_call_target="tpu_custom_call" | custom-call | tf_op jit(solution)/shard_map/pallas_call | solution.py:336
  42.0 1.0 %copy.6 = bf16[40,8,8,128]{3,2,1,0:T(8,128)(2,1)} copy(bf16[40,8,8,128]{3,1,2,0:T(8,128)(2,1)S(1)} %bitcast.6) | data formatting | bytes 1310720
Async XLA Ops:
  0.0 1.4 %copy-start = (bf16[64,216]{1,0:T(8,128)(2,1)S(1)}, bf16[64,216]{1,0:T(8,128)(2,1)}, u32[]{:S(2)}) copy-start(bf16[64,216]{1,0:T(8,128)(2,1)} %w_out_ref.1) | copy-start | bytes 82948
  0.0 1.4 %copy-start.3 = (bf16[24,576]{1,0:T(8,128)(2,1)S(1)}, bf16[24,576]{1,0:T(8,128)(2,1)}, u32[]{:S(2)}) copy-start(bf16[24,576]{1,0:T(8,128)(2,1)} %wv_ref.1) | copy-start | bytes 82948
  0.0 1.4 %copy-start.2 = (bf16[24,576]{1,0:T(8,128)(2,1)S(1)}, bf16[24,576]{1,0:T(8,128)(2,1)}, u32[]{:S(2)}) copy-start(bf16[24,576]{1,0:T(8,128)(2,1)} %wk_ref.1) | copy-start | bytes 82948
  0.0 1.4 %copy-start.1 = (bf16[24,576]{1,0:T(8,128)(2,1)S(1)}, bf16[24,576]{1,0:T(8,128)(2,1)}, u32[]{:S(2)}) copy-start(bf16[24,576]{1,0:T(8,128)(2,1)} %wq_ref.1) | copy-start | bytes 82948

commit v2 on v1

--- a/solution.py
+++ b/solution.py
@@ -205,8 +205,7 @@
             v_copies[t, k] = remote(
                 v_all.at[t, z], v_all.at[t, z], v_s.at[t, k], v_r.at[t, z], {"mem": far_peer(k)}
             )
-    for k in range(mems - 1):
-        v_copies[order[0], k].start()
+    v_copies[order[0], 0].start()
 
     column = lax.broadcasted_iota(jnp.int32, (cq, total * cq), 1).astype(F32)
     row = lax.broadcasted_iota(jnp.int32, (cq, total * cq), 0).astype(F32)
@@ -251,8 +250,8 @@
     ]
     for copy in gm_copies:
         copy.start()
-    for t in order[1:]:
-        for k in range(mems - 1):
+    for t in order:
+        for k in range(1 if t == order[0] else 0, mems - 1):
             v_copies[t, k].start()
     g_mem[z] = g_out[z]
     for copy in gm_copies:

time: 43.1 us -> 43.3 us (level)
  no operation moved by 1% of the time
where the time goes in v2:
time: 43.3 us; the launch traced here: 43.2 us
  Pallas kernels  40.8 us (94%)
  local copies, waits for them, and re-layouts  2.36 us (5%)
    pallas_call x1, Pallas kernels, shards(): pl.pallas_call(functools.partial(layer_kernel, dims), out_shape=jax.Shape...  40.8 us
    reshape x1, local copies, waits for them, and re-layouts, shards(): fields.reshape(members, ch, wide)  1.39 us
    unnamed x9, local copies, waits for them, and re-layouts  0.98 us

profile of v2, /device:TPU:0, one launch (start us, length us, event | category | flops | bytes accessed | tf_op | source)
XLA Modules:
  0.0 43.2 jit_solution(13297229287715654701)
XLA Ops:
  0.0 0.0 copy-start
  0.0 0.0 copy-start.3
  0.0 0.0 copy-start.2
  0.0 0.0 copy-start.1
  0.0 1.4 %reshape.6.f_ref = bf16[5,64,1024]{2,1,0:T(8,128)(2,1)S(1)} reshape(bf16[5,64,8,128]{3,2,1,0:T(8,128)(2,1)} %param.5) | data formatting | bytes 1310720 | tf_op jit(solution)/shard_map/reshape | solution.py:366
  1.4 0.0 copy-done
  1.4 0.0 copy-done.3
  1.4 0.0 copy-done.2
  1.4 0.0 copy-done.1
  1.4 40.8 %shard_map.55 = bf16[5,64,1024]{2,1,0:T(8,128)(2,1)S(1)} custom-call(bf16[5,64,1024]{2,1,0:T(8,128)(2,1)S(1)} %reshape.6.f_ref, bf16[24,576]{1,0:T(8,128)(2,1)S(1)} %copy-done.1, bf16[24,576]{1,0:T(8,128)(2,1)S(1)} %copy-done.2, bf16[24,576]{1,0:T(8,128)(2,1)S(1)} %copy-done.3, bf16[64,216]{1,0:T(8,128)(2,1)S(1)} %copy-done), custom_call_target="tpu_custom_call" | custom-call | tf_op jit(solution)/shard_map/pallas_call | solution.py:335
  42.2 1.0 %copy.6 = bf16[40,8,8,128]{3,2,1,0:T(8,128)(2,1)} copy(bf16[40,8,8,128]{3,1,2,0:T(8,128)(2,1)S(1)} %bitcast.6) | data formatting | bytes 1310720
Async XLA Ops:
  0.0 1.4 %copy-start = (bf16[64,216]{1,0:T(8,128)(2,1)S(1)}, bf16[64,216]{1,0:T(8,128)(2,1)}, u32[]{:S(2)}) copy-start(bf16[64,216]{1,0:T(8,128)(2,1)} %w_out_ref.1) | copy-start | bytes 82948
  0.0 1.4 %copy-start.3 = (bf16[24,576]{1,0:T(8,128)(2,1)S(1)}, bf16[24,576]{1,0:T(8,128)(2,1)}, u32[]{:S(2)}) copy-start(bf16[24,576]{1,0:T(8,128)(2,1)} %wv_ref.1) | copy-start | bytes 82948
  0.0 1.4 %copy-start.2 = (bf16[24,576]{1,0:T(8,128)(2,1)S(1)}, bf16[24,576]{1,0:T(8,128)(2,1)}, u32[]{:S(2)}) copy-start(bf16[24,576]{1,0:T(8,128)(2,1)} %wk_ref.1) | copy-start | bytes 82948
  0.0 1.4 %copy-start.1 = (bf16[24,576]{1,0:T(8,128)(2,1)S(1)}, bf16[24,576]{1,0:T(8,128)(2,1)}, u32[]{:S(2)}) copy-start(bf16[24,576]{1,0:T(8,128)(2,1)} %wq_ref.1) | copy-start | bytes 82948
